TPU v7x, 512 devices: a whole 4x4x16 slice. The times are simulated.
512 devices in a mesh: pipe: 16 (over z), blk: 32 (over x, y, core).
Axes of the slice: x: 4, y: 4, z: 16, core: 2. Of those that a mesh axis runs over, the one named last changes fastest.
Arguments:
- stream: bfloat16 [16, 128, 6144], P('pipe', 'blk'), may hold values from -6 to 6
- arrivals: bfloat16 [3, 128, 6144], P(None, 'blk'), may hold values from -6 to 6
- ln_gain: bfloat16 [16, 6144], P('pipe'), may hold values from 0.099609375 to 1.8984375
- ln_bias: bfloat16 [16, 6144], P('pipe'), may hold values from -3 to 3
- up_weight: bfloat16 [16, 6144, 4096], P('pipe', None, 'blk'), may hold values from -0.078125 to 0.078125
- up_bias: bfloat16 [16, 4096], P('pipe', 'blk'), may hold values from -3 to 3
- down_weight: bfloat16 [16, 4096, 6144], P('pipe', 'blk'), may hold values from -0.1875 to 0.1875
- down_bias: bfloat16 [16, 6144], P('pipe'), may hold values from -3 to 3
- active: int32 [4, 16, 2, 16], P(None, 'pipe'), may hold values from -1 to 31, as said below
Outputs:
- passed: bfloat16 [16, 4, 128, 6144], P('pipe', None, 'blk')
Inputs may be any that keep to these rules, and one draw needn't show every extreme that they name: Each list holds between 8 and 16 distinct block ids, followed by -1 padding; some blocks are active far more often than others.
All inputs are finite; a program needn't handle non-finite values.
Results may differ from a plain program's by a relative error of at most 0.019.
Values may be sent and summed in bfloat16 or wider, within the bound.
No kernel may reach another device: no remote copies, remote signals or barrier semaphores. Data moves between devices by JAX's collectives and lax.ppermute only.
A program may use at most 64 MiB of HBM per device.

v0:
```python
import jax
import jax.numpy as jnp
from jax import lax
from jax.sharding import PartitionSpec as P

TILE = 64
TICKS = 4


def shifted(block, axis, distance):
    devices = range(lax.axis_size(axis))
    route = [(i - distance, i) for i in devices if i - distance in devices]
    return lax.ppermute(block, axis, route)


def layer_norm(rows, gain_row, shift_row):
    widened = rows.astype(jnp.float32)
    row_mean = jnp.mean(widened, axis=-1, keepdims=True)
    centred = widened - row_mean
    row_var = jnp.mean(centred * centred, axis=-1, keepdims=True)
    scaled = centred * lax.rsqrt(row_var + 1e-05)
    return (scaled * gain_row + shift_row).astype(jnp.bfloat16)


def on_device(
    stream, arrivals, ln_gain, ln_bias, up_weight, up_bias, down_weight, down_bias, active
):
    blocks = lax.axis_size("blk")
    my_index = lax.axis_index("blk")
    section = lax.axis_index("pipe")
    rows_dev = stream.shape[1]
    width = stream.shape[2]
    w_up = up_weight[0]
    b_up = up_bias[0].astype(jnp.float32)
    w_down = down_weight[0]
    gain_row = ln_gain[0].astype(jnp.float32)
    shift_row = ln_bias[0].astype(jnp.float32)
    b_down = down_bias[0].astype(jnp.float32)
    current = stream[0]
    results = []
    for step_index in range(TICKS):
        tile_lists = active[step_index, 0]
        tile_count = tile_lists.shape[0]
        owned_tiles = jnp.any(tile_lists == my_index, axis=1).astype(jnp.float32)
        normed = layer_norm(current, gain_row, shift_row)
        piece = lax.all_gather(normed, "blk", axis=0, tiled=True)
        row_index = jnp.arange(piece.shape[0], dtype=jnp.int32)
        matches = row_index[:, None] // TILE == jnp.arange(tile_count, dtype=jnp.int32)[None, :]
        row_flag = jnp.sum(matches.astype(jnp.float32) * owned_tiles[None, :], axis=1)
        preact = jnp.dot(piece, w_up, preferred_element_type=jnp.float32) + b_up
        activity = (jnp.maximum(preact, 0.0) * row_flag[:, None]).astype(jnp.bfloat16)
        partials = jnp.dot(activity, w_down, preferred_element_type=jnp.float32).astype(
            jnp.bfloat16
        )
        stacked = partials.reshape(blocks, rows_dev, width)
        received = lax.all_to_all(stacked, "blk", split_axis=0, concat_axis=0, tiled=True)
        summed = jnp.sum(received.astype(jnp.float32), axis=0)
        produced = (current.astype(jnp.float32) + summed + b_down).astype(jnp.bfloat16)
        results.append(produced)
        if step_index + 1 < TICKS:
            moved = shifted(produced, "pipe", 1)
            current = jnp.where(section == 0, arrivals[step_index], moved)
    return jnp.stack(results)[None]


def solution(mesh):
    return jax.shard_map(
        on_device,
        mesh=mesh,
        in_specs=(
            P("pipe", "blk", None),
            P(None, "blk", None),
            P("pipe", None),
            P("pipe", None),
            P("pipe", None, "blk"),
            P("pipe", "blk"),
            P("pipe", "blk", None),
            P("pipe", None),
            P(None, "pipe", None, None),
        ),
        out_specs=P("pipe", None, "blk", None),
        check_vma=False,
    )
```

profile of v0, /device:TPU:1, one launch (start us, length us, event | category | flops | bytes accessed | tf_op | source)
XLA Modules:
  0.0 441.8 jit_solution(18012084157302393708)
XLA Ops:
  13.4 62.7 %all-gather.9.cloned.1.call-done = bf16[32,4,6144]{2,1,0:T(4,128)(2,1)} async-done(((bf16[1,4,6144]{2,1,0:T(4,128)(2,1)}), bf16[32,4,6144]{2,1,0:T(4,128)(2,1)}) %all-gather.9.cloned.1.call-update) | async-done | bytes 1572880 | tf_op jit(solution)/shard_map/all_gather | solution.py:46
  76.2 3.7 reshape.139
  79.9 3.6 convolution_convert_fusion.3
  83.5 3.8 reshape.130
  87.3 5.4 %all-to-all-start = ((bf16[32,4,6144]{2,1,0:T(4,128)(2,1)}), bf16[32,4,6144]{2,1,0:T(4,128)(2,1)}, u32[]{:S(2)}, u32[]{:S(2)}) async-start(bf16[32,4,6144]{2,1,0:T(4,128)(2,1)} %reshape.130), calls=%async_computation | async-start | bytes 3145728 | tf_op jit(solution)/shard_map/all_to_all | solution.py:56
  92.8 22.6 %all-to-all-done = bf16[32,4,6144]{2,1,0:T(4,128)(2,1)} async-done(((bf16[32,4,6144]{2,1,0:T(4,128)(2,1)}), bf16[32,4,6144]{2,1,0:T(4,128)(2,1)}, u32[]{:S(2)}, u32[]{:S(2)}) %all-to-all-start) | async-done | bytes 1572896 | tf_op jit(solution)/shard_map/all_to_all | solution.py:56
  117.6 3.2 collective-permute-start
  123.9 59.6 %all-gather.11.cloned.1.call-done = bf16[32,4,6144]{2,1,0:T(4,128)(2,1)} async-done(((bf16[1,4,6144]{2,1,0:T(4,128)(2,1)}), bf16[32,4,6144]{2,1,0:T(4,128)(2,1)}) %all-gather.11.cloned.1.call-update) | async-done | bytes 1572880 | tf_op jit(solution)/shard_map/all_gather | solution.py:46
  183.5 3.7 reshape.141
  187.2 3.6 convolution_convert_fusion.2
  190.8 3.8 reshape.131
  194.6 28.1 %all_to_all.20 = bf16[32,4,6144]{2,1,0:T(4,128)(2,1)S(1)} all-to-all(bf16[32,4,6144]{2,1,0:T(4,128)(2,1)} %reshape.131), channel_id=1, replica_groups=mesh['pipe'=16,'blk'=32] {'blk'}, dimensions={0} | all-to-all | bytes 3145728 | tf_op jit(solution)/shard_map/all_to_all | solution.py:56
  223.4 3.2 collective-permute-start.1
  229.9 59.2 %all-gather.13.cloned.1.call-done = bf16[32,4,6144]{2,1,0:T(4,128)(2,1)} async-done(((bf16[1,4,6144]{2,1,0:T(4,128)(2,1)}), bf16[32,4,6144]{2,1,0:T(4,128)(2,1)}) %all-gather.13.cloned.1.call-update) | async-done | bytes 1572880 | tf_op jit(solution)/shard_map/all_gather | solution.py:46
  289.1 3.7 reshape.143
  292.8 3.6 convolution_convert_fusion.1
  296.4 3.8 reshape.132
  300.2 28.1 %all_to_all.21 = bf16[32,4,6144]{2,1,0:T(4,128)(2,1)S(1)} all-to-all(bf16[32,4,6144]{2,1,0:T(4,128)(2,1)} %reshape.132), channel_id=1, replica_groups=mesh['pipe'=16,'blk'=32] {'blk'}, dimensions={0} | all-to-all | bytes 3145728 | tf_op jit(solution)/shard_map/all_to_all | solution.py:56
  335.4 59.3 %all-gather.15.cloned.1.call-done = bf16[32,4,6144]{2,1,0:T(4,128)(2,1)} async-done(((bf16[1,4,6144]{2,1,0:T(4,128)(2,1)}), bf16[32,4,6144]{2,1,0:T(4,128)(2,1)}) %all-gather.15.cloned.1.call-update) | async-done | bytes 1572880 | tf_op jit(solution)/shard_map/all_gather | solution.py:46
  394.7 3.7 reshape.145
  398.4 3.6 convolution_convert_fusion
  402.0 3.8 reshape.133
  405.8 5.2 %all-to-all-start.3 = ((bf16[32,4,6144]{2,1,0:T(4,128)(2,1)}), bf16[32,4,6144]{2,1,0:T(4,128)(2,1)S(1)}, u32[]{:S(2)}, u32[]{:S(2)}) async-start(bf16[32,4,6144]{2,1,0:T(4,128)(2,1)} %reshape.133), calls=%async_computation.3 | async-start | bytes 3145728 | tf_op jit(solution)/shard_map/all_to_all | solution.py:56
  411.1 22.6 %all-to-all-done.3 = bf16[32,4,6144]{2,1,0:T(4,128)(2,1)S(1)} async-done(((bf16[32,4,6144]{2,1,0:T(4,128)(2,1)}), bf16[32,4,6144]{2,1,0:T(4,128)(2,1)S(1)}, u32[]{:S(2)}, u32[]{:S(2)}) %all-to-all-start.3) | async-done | bytes 1572896 | tf_op jit(solution)/shard_map/all_to_all | solution.py:56
  (61 shorter events, 24.9 us)
Async XLA Ops:
  6.5 73.3 %copy-start = (bf16[1,128,6144]{2,1,0:T(8,128)(2,1)S(1)}, bf16[1,128,6144]{2,1,0:T(8,128)(2,1)}, u32[]{:S(2)}) copy-start(bf16[1,128,6144]{2,1,0:T(8,128)(2,1)} %param.15) | copy-start | bytes 4718596
  6.5 69.7 %all-gather.9.cloned.1.call-start = ((), (), s32[]{:S(2)}) async-start(), calls=%async_computation.4 | async-start | bytes 1622016 | tf_op jit(solution)/shard_map/all_gather | solution.py:46
  13.4 66.4 %copy-start.1 = (bf16[1,6144,128]{2,1,0:T(8,128)(2,1)S(1)}, bf16[1,6144,128]{2,1,0:T(8,128)(2,1)}, u32[]{:S(2)}) copy-start(bf16[1,6144,128]{2,1,0:T(8,128)(2,1)} %param.13) | copy-start | bytes 4718596
  87.3 5.5 %copy-start.3 = (bf16[1,6144]{1,0:T(2,128)(2,1)S(1)}, bf16[1,6144]{1,0:T(2,128)(2,1)}, u32[]{:S(2)}) copy-start(bf16[1,6144]{1,0:T(2,128)(2,1)} %param.16) | copy-start | bytes 36868
  87.3 28.1 %all-to-all-start = ((bf16[32,4,6144]{2,1,0:T(4,128)(2,1)}), bf16[32,4,6144]{2,1,0:T(4,128)(2,1)}, u32[]{:S(2)}, u32[]{:S(2)}) async-start(bf16[32,4,6144]{2,1,0:T(4,128)(2,1)} %reshape.130), calls=%async_computation | async-start | bytes 3145728 | tf_op jit(solution)/shard_map/all_to_all | solution.py:56
  92.7 24.8 %copy-start.2 = (bf16[1,4,6144]{2,1,0:T(4,128)(2,1)S(1)}, bf16[1,4,6144]{2,1,0:T(4,128)(2,1)}, u32[]{:S(2)}) copy-start(bf16[1,4,6144]{2,1,0:T(4,128)(2,1)} %param.9) | copy-start | bytes 147460
  92.7 90.8 %all-gather.11.cloned.1.call-start = ((), (), s32[]{:S(2)}) async-start(), calls=%async_computation.5 | async-start | bytes 1622016 | tf_op jit(solution)/shard_map/all_gather | solution.py:46
  117.6 4.3 collective-permute-start
  123.9 165.2 %all-gather.13.cloned.1.call-start = ((), (), s32[]{:S(2)}) async-start(), calls=%async_computation.6 | async-start | bytes 1622016 | tf_op jit(solution)/shard_map/all_gather | solution.py:46
  223.4 4.5 %collective-permute-start.1 = (bf16[4,6144]{1,0:T(4,128)(2,1)S(1)}, bf16[4,6144]{1,0:T(4,128)(2,1)S(1)}, u32[]{:S(2)}, u32[]{:S(2)}) collective-permute-start(bf16[4,6144]{1,0:T(4,128)(2,1)S(1)} %fusion.99), channel_id=1, source_target_pairs={{0,32},{32,64},{64,96},{96,128},{128,160},{160,192},{192,224},{224... | collective-permute-start | bytes 147464 | tf_op jit(solution)/shard_map/ppermute | solution.py:13
  229.9 164.8 %all-gather.15.cloned.1.call-start = ((), (), s32[]{:S(2)}) async-start(), calls=%async_computation.7 | async-start | bytes 1622016 | tf_op jit(solution)/shard_map/all_gather | solution.py:46
  329.0 4.5 %collective-permute-start.2 = (bf16[4,6144]{1,0:T(4,128)(2,1)S(1)}, bf16[4,6144]{1,0:T(4,128)(2,1)S(1)}, u32[]{:S(2)}, u32[]{:S(2)}) collective-permute-start(bf16[4,6144]{1,0:T(4,128)(2,1)S(1)} %fusion.101), channel_id=1, source_target_pairs={{0,32},{32,64},{64,96},{96,128},{128,160},{160,192},{192,224},{224... | collective-permute-start | bytes 147464 | tf_op jit(solution)/shard_map/ppermute | solution.py:13
  405.8 27.9 %all-to-all-start.3 = ((bf16[32,4,6144]{2,1,0:T(4,128)(2,1)}), bf16[32,4,6144]{2,1,0:T(4,128)(2,1)S(1)}, u32[]{:S(2)}, u32[]{:S(2)}) async-start(bf16[32,4,6144]{2,1,0:T(4,128)(2,1)} %reshape.133), calls=%async_computation.3 | async-start | bytes 3145728 | tf_op jit(solution)/shard_map/all_to_all | solution.py:56
Sparse Core Ops, SparseCore 0:
  11.9 64.2 all-gather.8
  124.0 59.4 all-gather.10
  230.0 59.0 all-gather.12
  335.6 59.0 all-gather.14
where the time goes:
time: 443 us; the launch traced here: 442 us
  waiting for transfers between devices  290 us (65%)
  blocking collectives  56.1 us (13%)
  local copies, waits for them, and re-layouts  29.9 us (7%)
  starting transfers between devices  20.3 us (5%)
  other arithmetic  17.7 us (4%)
  matrix products  14.5 us (3%)
  between operations  13.3 us (3%)
    all_gather x4, waiting for transfers between devices, on_device(): piece = lax.all_gather(normed, 'blk', axis=0, tiled=True)  241 us
    all_to_all x2, blocking collectives, on_device(): lax.all_to_all(stacked, 'blk', split_axis=0, concat_axis=0, tiled=True)  56.1 us
    all_to_all x2, waiting for transfers between devices, on_device(): lax.all_to_all(stacked, 'blk', split_axis=0, concat_axis=0, tiled=True)  45.3 us
    reshape x4, local copies, waits for them, and re-layouts, on_device(): stacked = partials.reshape(blocks, rows_dev, width)  15.2 us
    unnamed x12, local copies, waits for them, and re-layouts  14.7 us
    dot_general x4, matrix products, on_device(): jnp.dot(activity, w_down, preferred_element_type=jnp.float32)  14.5 us
    all_to_all x2, starting transfers between devices, on_device(): lax.all_to_all(stacked, 'blk', split_axis=0, concat_axis=0, tiled=True)  10.6 us
    ppermute x3, starting transfers between devices, shifted(): return lax.ppermute(block, axis, route)  9.54 us
  transfers between devices with their start and end apart: 9, of which 9 were waited for; matrix products, arithmetic and copies ran while one was open for 0% of the time, Pallas kernels for 0%

commit v1 on v0

--- a/solution.py
+++ b/solution.py
@@ -43,7 +43,9 @@
         tile_count = tile_lists.shape[0]
         owned_tiles = jnp.any(tile_lists == my_index, axis=1).astype(jnp.float32)
         normed = layer_norm(current, gain_row, shift_row)
-        piece = lax.all_gather(normed, "blk", axis=0, tiled=True)
+        piece = jnp.concatenate(
+            lax.all_to_all(jnp.stack([normed] * lax.axis_size("blk")), "blk", 0, 0), axis=0
+        )
         row_index = jnp.arange(piece.shape[0], dtype=jnp.int32)
         matches = row_index[:, None] // TILE == jnp.arange(tile_count, dtype=jnp.int32)[None, :]
         row_flag = jnp.sum(matches.astype(jnp.float32) * owned_tiles[None, :], axis=1)

time: 443 us -> 303 us (0.68)
  waiting for transfers between devices: 290 us -> 71.5 us
  blocking collectives: 56.1 us -> 135 us
  between operations: 13.3 us -> 0.27 us
  starting transfers between devices: 20.3 us -> 29.4 us
    all_gather x4 -> x0, waiting for transfers between devices: 241 us -> none  [on_device(): piece = lax.all_gather(normed, 'blk', axis=0, tiled=True)]
    all_to_all x0 -> x3, blocking collectives: none -> 81.7 us  [on_device(): lax.all_to_all(jnp.stack([normed] * lax.axis_size('blk')), 'blk', 0, 0)]
    all_to_all x0 -> x1, waiting for transfers between devices: none -> 22.5 us  [on_device(): lax.all_to_all(jnp.stack([normed] * lax.axis_size('blk')), 'blk', 0, 0)]
    unnamed x12, local copies, waits for them, and re-layouts: 14.7 us -> 0.03 us
    reshape x0 -> x4, local copies, waits for them, and re-layouts: none -> 14.6 us  [on_device(): jnp.concatenate(lax.all_to_all(jnp.stack([normed] * lax.axis_size('blk'))...]
    all_to_all x0 -> x1, starting transfers between devices: none -> 11.3 us  [on_device(): lax.all_to_all(jnp.stack([normed] * lax.axis_size('blk')), 'blk', 0, 0)]
  transfers between devices with their start and end apart: 9 -> 6, of which waited for: 9 -> 6; matrix products, arithmetic and copies ran while one was open for 0% -> 0% of each run, Pallas kernels for 0% -> 0%
where the time goes in v1:
time: 303 us; the launch traced here: 298 us
  blocking collectives  135 us (45%)
  waiting for transfers between devices  71.5 us (24%)
  local copies, waits for them, and re-layouts  33.8 us (11%)
  starting transfers between devices  29.4 us (10%)
  matrix products  14.5 us (5%)
  other arithmetic  13.9 us (5%)
    all_to_all x3, blocking collectives, on_device(): lax.all_to_all(jnp.stack([normed] * lax.axis_size('blk')), 'blk', 0, 0)  81.7 us
    all_to_all x2, blocking collectives, on_device(): lax.all_to_all(stacked, 'blk', split_axis=0, concat_axis=0, tiled=True)  52.9 us
    all_to_all x2, waiting for transfers between devices, on_device(): lax.all_to_all(stacked, 'blk', split_axis=0, concat_axis=0, tiled=True)  45.3 us
    all_to_all x1, waiting for transfers between devices, on_device(): lax.all_to_all(jnp.stack([normed] * lax.axis_size('blk')), 'blk', 0, 0)  22.5 us
    reshape x4, local copies, waits for them, and re-layouts, on_device(): stacked = partials.reshape(blocks, rows_dev, width)  15.2 us
    reshape x4, local copies, waits for them, and re-layouts, on_device(): jnp.concatenate(lax.all_to_all(jnp.stack([normed] * lax.axis_size('blk'))...  14.6 us
    dot_general x4, matrix products, on_device(): jnp.dot(activity, w_down, preferred_element_type=jnp.float32)  14.5 us
    all_to_all x1, starting transfers between devices, on_device(): lax.all_to_all(jnp.stack([normed] * lax.axis_size('blk')), 'blk', 0, 0)  11.3 us
  transfers between devices with their start and end apart: 6, of which 6 were waited for; matrix products, arithmetic and copies ran while one was open for 0% of the time, Pallas kernels for 0%

profile of v1, /device:TPU:1, one launch (start us, length us, event | category | flops | bytes accessed | tf_op | source)
XLA Modules:
  0.0 298.1 jit_solution(13997418362415670369)
XLA Ops:
  6.4 11.3 %all-to-all-start = ((bf16[32,4,6144]{2,1,0:T(4,128)(2,1)}), bf16[32,4,6144]{2,1,0:T(4,128)(2,1)}, u32[]{:S(2)}, u32[]{:S(2)}) async-start(bf16[32,4,6144]{2,1,0:T(4,128)(2,1)} %stack.19), calls=%async_computation | async-start | bytes 3145728 | tf_op jit(solution)/shard_map/all_to_all | solution.py:47
  18.1 22.5 %all-to-all-done = bf16[32,4,6144]{2,1,0:T(4,128)(2,1)} async-done(((bf16[32,4,6144]{2,1,0:T(4,128)(2,1)}), bf16[32,4,6144]{2,1,0:T(4,128)(2,1)}, u32[]{:S(2)}, u32[]{:S(2)}) %all-to-all-start) | async-done | bytes 1572896 | tf_op jit(solution)/shard_map/all_to_all | solution.py:47
  40.6 3.6 %reshape.177 = bf16[128,6144]{1,0:T(8,128)(2,1)} reshape(bf16[32,4,6144]{2,1,0:T(4,128)(2,1)} %all-to-all-done) | data formatting | bytes 3145728 | tf_op jit(solution)/shard_map/reshape | solution.py:46
  44.2 3.6 %convolution_convert_fusion.3 = bf16[128,6144]{1,0:T(8,128)(2,1)} fusion(bf16[1,128,6144]{2,1,0:T(8,128)(2,1)S(1)} %copy-done, bf16[128,6144]{1,0:T(8,128)(2,1)} %reshape.177, bf16[1,6144,128]{2,1,0:T(8,128)(2,1)S(1)} %copy-done.1, f32[128]{0:T(128)S(1)} %get-tuple-element.12, f32[128]{0:T(128)S(1)} %bitcast_convert_fusion), kind=kOutput, calls=%fused_computation.3 | convolution fusion | flops 403505152 | bytes 6292480 | tf_op jit(solution)/shard_map/dot_general | solution.py:54
  47.9 3.8 %reshape.178 = bf16[32,4,6144]{2,1,0:T(4,128)(2,1)} reshape(bf16[128,6144]{1,0:T(8,128)(2,1)} %convolution_convert_fusion.3) | data formatting | bytes 3145728 | tf_op jit(solution)/shard_map/reshape | solution.py:57
  51.7 5.1 %all-to-all-start.1 = ((bf16[32,4,6144]{2,1,0:T(4,128)(2,1)}), bf16[32,4,6144]{2,1,0:T(4,128)(2,1)}, u32[]{:S(2)}, u32[]{:S(2)}) async-start(bf16[32,4,6144]{2,1,0:T(4,128)(2,1)} %reshape.178), calls=%async_computation.1 | async-start | bytes 3145728 | tf_op jit(solution)/shard_map/all_to_all | solution.py:58
  56.8 22.8 %all-to-all-done.1 = bf16[32,4,6144]{2,1,0:T(4,128)(2,1)} async-done(((bf16[32,4,6144]{2,1,0:T(4,128)(2,1)}), bf16[32,4,6144]{2,1,0:T(4,128)(2,1)}, u32[]{:S(2)}, u32[]{:S(2)}) %all-to-all-start.1) | async-done | bytes 1572896 | tf_op jit(solution)/shard_map/all_to_all | solution.py:58
  86.2 27.6 %all_to_all.40 = bf16[32,4,6144]{2,1,0:T(4,128)(2,1)} all-to-all(bf16[32,4,6144]{2,1,0:T(4,128)(2,1)S(1)} %stack.20), channel_id=1, replica_groups=mesh['pipe'=16,'blk'=32] {'blk'}, dimensions={0} | all-to-all | bytes 3145728 | tf_op jit(solution)/shard_map/all_to_all | solution.py:47
  113.8 3.7 %reshape.179 = bf16[128,6144]{1,0:T(8,128)(2,1)} reshape(bf16[32,4,6144]{2,1,0:T(4,128)(2,1)} %all_to_all.40) | data formatting | bytes 3145728 | tf_op jit(solution)/shard_map/reshape | solution.py:46
  117.5 3.6 %convolution_convert_fusion.2 = bf16[128,6144]{1,0:T(8,128)(2,1)} fusion(bf16[1,128,6144]{2,1,0:T(8,128)(2,1)S(1)} %copy-done, bf16[128,6144]{1,0:T(8,128)(2,1)} %reshape.179, bf16[1,6144,128]{2,1,0:T(8,128)(2,1)S(1)} %copy-done.1, f32[128]{0:T(128)S(1)} %get-tuple-element.11, f32[128]{0:T(128)S(1)} %bitcast_convert_fusion), kind=kOutput, calls=%fused_computation.2 | convolution fusion | flops 403505152 | bytes 6292480 | tf_op jit(solution)/shard_map/dot_general | solution.py:54
  121.1 3.8 %reshape.180 = bf16[32,4,6144]{2,1,0:T(4,128)(2,1)} reshape(bf16[128,6144]{1,0:T(8,128)(2,1)} %convolution_convert_fusion.2) | data formatting | bytes 3145728 | tf_op jit(solution)/shard_map/reshape | solution.py:57
  124.9 26.4 %all_to_all.41 = bf16[32,4,6144]{2,1,0:T(4,128)(2,1)S(1)} all-to-all(bf16[32,4,6144]{2,1,0:T(4,128)(2,1)} %reshape.180), channel_id=1, replica_groups=mesh['pipe'=16,'blk'=32] {'blk'}, dimensions={0} | all-to-all | bytes 3145728 | tf_op jit(solution)/shard_map/all_to_all | solution.py:58
  152.0 4.0 %collective-permute-start.1 = (bf16[4,6144]{1,0:T(4,128)(2,1)S(1)}, bf16[4,6144]{1,0:T(4,128)(2,1)S(1)}, u32[]{:S(2)}, u32[]{:S(2)}) collective-permute-start(bf16[4,6144]{1,0:T(4,128)(2,1)S(1)} %fusion.93), channel_id=1, source_target_pairs={{0,32},{32,64},{64,96},{96,128},{128,160},{160,192},{192,224},{224... | collective-permute-start | bytes 147464 | tf_op jit(solution)/shard_map/ppermute | solution.py:13
  159.4 27.1 %all_to_all.42 = bf16[32,4,6144]{2,1,0:T(4,128)(2,1)} all-to-all(bf16[32,4,6144]{2,1,0:T(4,128)(2,1)S(1)} %stack.22), channel_id=1, replica_groups=mesh['pipe'=16,'blk'=32] {'blk'}, dimensions={0} | all-to-all | bytes 3145728 | tf_op jit(solution)/shard_map/all_to_all | solution.py:47
  186.4 3.7 %reshape.181 = bf16[128,6144]{1,0:T(8,128)(2,1)} reshape(bf16[32,4,6144]{2,1,0:T(4,128)(2,1)} %all_to_all.42) | data formatting | bytes 3145728 | tf_op jit(solution)/shard_map/reshape | solution.py:46
  193.7 3.8 %reshape.182 = bf16[32,4,6144]{2,1,0:T(4,128)(2,1)} reshape(bf16[128,6144]{1,0:T(8,128)(2,1)} %convolution_convert_fusion.1) | data formatting | bytes 3145728 | tf_op jit(solution)/shard_map/reshape | solution.py:57
  197.5 26.5 %all_to_all.43 = bf16[32,4,6144]{2,1,0:T(4,128)(2,1)S(1)} all-to-all(bf16[32,4,6144]{2,1,0:T(4,128)(2,1)} %reshape.182), channel_id=1, replica_groups=mesh['pipe'=16,'blk'=32] {'blk'}, dimensions={0} | all-to-all | bytes 3145728 | tf_op jit(solution)/shard_map/all_to_all | solution.py:58
  224.7 4.0 %collective-permute-start.2 = (bf16[4,6144]{1,0:T(4,128)(2,1)S(1)}, bf16[4,6144]{1,0:T(4,128)(2,1)S(1)}, u32[]{:S(2)}, u32[]{:S(2)}) collective-permute-start(bf16[4,6144]{1,0:T(4,128)(2,1)S(1)} %fusion.95), channel_id=1, source_target_pairs={{0,32},{32,64},{64,96},{96,128},{128,160},{160,192},{192,224},{224... | collective-permute-start | bytes 147464 | tf_op jit(solution)/shard_map/ppermute | solution.py:13
  232.1 27.1 %all_to_all.44 = bf16[32,4,6144]{2,1,0:T(4,128)(2,1)} all-to-all(bf16[32,4,6144]{2,1,0:T(4,128)(2,1)S(1)} %stack.24), channel_id=1, replica_groups=mesh['pipe'=16,'blk'=32] {'blk'}, dimensions={0} | all-to-all | bytes 3145728 | tf_op jit(solution)/shard_map/all_to_all | solution.py:47
  259.1 3.7 %reshape.183 = bf16[128,6144]{1,0:T(8,128)(2,1)} reshape(bf16[32,4,6144]{2,1,0:T(4,128)(2,1)} %all_to_all.44) | data formatting | bytes 3145728 | tf_op jit(solution)/shard_map/reshape | solution.py:46
  262.8 3.6 %convolution_convert_fusion = bf16[128,6144]{1,0:T(8,128)(2,1)} fusion(bf16[1,128,6144]{2,1,0:T(8,128)(2,1)S(1)} %copy-done, bf16[128,6144]{1,0:T(8,128)(2,1)} %reshape.183, bf16[1,6144,128]{2,1,0:T(8,128)(2,1)S(1)} %copy-done.1, f32[128]{0:T(128)S(1)} %get-tuple-element.9, f32[128]{0:T(128)S(1)} %bitcast_convert_fusion), kind=kOutput, calls=%fused_computation | convolution fusion | flops 403505152 | bytes 6292480 | tf_op jit(solution)/shard_map/dot_general | solution.py:54
  266.4 3.8 %reshape.184 = bf16[32,4,6144]{2,1,0:T(4,128)(2,1)} reshape(bf16[128,6144]{1,0:T(8,128)(2,1)} %convolution_convert_fusion) | data formatting | bytes 3145728 | tf_op jit(solution)/shard_map/reshape | solution.py:57
  270.2 3.8 %all-to-all-start.7 = ((bf16[32,4,6144]{2,1,0:T(4,128)(2,1)}), bf16[32,4,6144]{2,1,0:T(4,128)(2,1)S(1)}, u32[]{:S(2)}, u32[]{:S(2)}) async-start(bf16[32,4,6144]{2,1,0:T(4,128)(2,1)} %reshape.184), calls=%async_computation.7 | async-start | bytes 3145728 | tf_op jit(solution)/shard_map/all_to_all | solution.py:58
  274.1 22.5 %all-to-all-done.7 = bf16[32,4,6144]{2,1,0:T(4,128)(2,1)S(1)} async-done(((bf16[32,4,6144]{2,1,0:T(4,128)(2,1)}), bf16[32,4,6144]{2,1,0:T(4,128)(2,1)S(1)}, u32[]{:S(2)}, u32[]{:S(2)}) %all-to-all-start.7) | async-done | bytes 1572896 | tf_op jit(solution)/shard_map/all_to_all | solution.py:58
  (62 shorter events, 26.6 us)
Async XLA Ops:
  0.0 44.2 %copy-start = (bf16[1,128,6144]{2,1,0:T(8,128)(2,1)S(1)}, bf16[1,128,6144]{2,1,0:T(8,128)(2,1)}, u32[]{:S(2)}) copy-start(bf16[1,128,6144]{2,1,0:T(8,128)(2,1)} %param.15) | copy-start | bytes 4718596
  6.4 11.3 %copy-start.4 = (s32[4,1,2,16]{3,2,1,0:T(2,128)S(1)}, s32[4,1,2,16]{3,2,1,0:T(2,128)}, u32[]{:S(2)}) copy-start(s32[4,1,2,16]{3,2,1,0:T(2,128)} %param.17) | copy-start | bytes 1540
  6.4 11.6 %copy-start.5 = (bf16[1,128]{1,0:T(2,128)(2,1)S(1)}, bf16[1,128]{1,0:T(2,128)(2,1)}, u32[]{:S(2)}) copy-start(bf16[1,128]{1,0:T(2,128)(2,1)} %param.14) | copy-start | bytes 772
  6.4 34.1 %all-to-all-start = ((bf16[32,4,6144]{2,1,0:T(4,128)(2,1)}), bf16[32,4,6144]{2,1,0:T(4,128)(2,1)}, u32[]{:S(2)}, u32[]{:S(2)}) async-start(bf16[32,4,6144]{2,1,0:T(4,128)(2,1)} %stack.19), calls=%async_computation | async-start | bytes 3145728 | tf_op jit(solution)/shard_map/all_to_all | solution.py:47
  18.1 26.1 %copy-start.1 = (bf16[1,6144,128]{2,1,0:T(8,128)(2,1)S(1)}, bf16[1,6144,128]{2,1,0:T(8,128)(2,1)}, u32[]{:S(2)}) copy-start(bf16[1,6144,128]{2,1,0:T(8,128)(2,1)} %param.13) | copy-start | bytes 4718596
  51.7 5.1 %copy-start.3 = (bf16[1,6144]{1,0:T(2,128)(2,1)S(1)}, bf16[1,6144]{1,0:T(2,128)(2,1)}, u32[]{:S(2)}) copy-start(bf16[1,6144]{1,0:T(2,128)(2,1)} %param.16) | copy-start | bytes 36868
  51.7 28.0 %all-to-all-start.1 = ((bf16[32,4,6144]{2,1,0:T(4,128)(2,1)}), bf16[32,4,6144]{2,1,0:T(4,128)(2,1)}, u32[]{:S(2)}, u32[]{:S(2)}) async-start(bf16[32,4,6144]{2,1,0:T(4,128)(2,1)} %reshape.178), calls=%async_computation.1 | async-start | bytes 3145728 | tf_op jit(solution)/shard_map/all_to_all | solution.py:58
  56.8 24.9 %copy-start.2 = (bf16[1,4,6144]{2,1,0:T(4,128)(2,1)S(1)}, bf16[1,4,6144]{2,1,0:T(4,128)(2,1)}, u32[]{:S(2)}) copy-start(bf16[1,4,6144]{2,1,0:T(4,128)(2,1)} %param.9) | copy-start | bytes 147460
  81.7 2.5 collective-permute-start
  152.0 5.3 %collective-permute-start.1 = (bf16[4,6144]{1,0:T(4,128)(2,1)S(1)}, bf16[4,6144]{1,0:T(4,128)(2,1)S(1)}, u32[]{:S(2)}, u32[]{:S(2)}) collective-permute-start(bf16[4,6144]{1,0:T(4,128)(2,1)S(1)} %fusion.93), channel_id=1, source_target_pairs={{0,32},{32,64},{64,96},{96,128},{128,160},{160,192},{192,224},{224... | collective-permute-start | bytes 147464 | tf_op jit(solution)/shard_map/ppermute | solution.py:13
  224.7 5.3 %collective-permute-start.2 = (bf16[4,6144]{1,0:T(4,128)(2,1)S(1)}, bf16[4,6144]{1,0:T(4,128)(2,1)S(1)}, u32[]{:S(2)}, u32[]{:S(2)}) collective-permute-start(bf16[4,6144]{1,0:T(4,128)(2,1)S(1)} %fusion.95), channel_id=1, source_target_pairs={{0,32},{32,64},{64,96},{96,128},{128,160},{160,192},{192,224},{224... | collective-permute-start | bytes 147464 | tf_op jit(solution)/shard_map/ppermute | solution.py:13
  270.2 26.3 %all-to-all-start.7 = ((bf16[32,4,6144]{2,1,0:T(4,128)(2,1)}), bf16[32,4,6144]{2,1,0:T(4,128)(2,1)S(1)}, u32[]{:S(2)}, u32[]{:S(2)}) async-start(bf16[32,4,6144]{2,1,0:T(4,128)(2,1)} %reshape.184), calls=%async_computation.7 | async-start | bytes 3145728 | tf_op jit(solution)/shard_map/all_to_all | solution.py:58
